TPU v7x, 32 devices: a whole 2x2x4 slice. The times are simulated.
32 devices in a mesh: rows: 16 (over z, y, x), rep: 2 (over core).
Axes of the slice: x: 2, y: 2, z: 4, core: 2. Of those that a mesh axis runs over, the one named last changes fastest.
Arguments:
- entity_table: bfloat16 [98304, 256], P('rows'), may hold values from -3 to 3
- relation_ops: bfloat16 [8, 256, 256], replicated, may hold values from -0.375 to 0.375
- need_rows: int32 [16, 2, 16, 8], P('rows', 'rep'), may hold values from 0 to 6143
- send_offsets: int32 [16, 2, 17], P('rows', 'rep'), may hold values from 0 to 128, as said below
- source_ids: int32 [16, 2, 2, 1024], P('rows', 'rep'), may hold values from 0 to 127, as said below
- target_ids: int32 [16, 2, 2, 1024], P('rows', 'rep'), may hold values from 0 to 127, as said below
- negative_ids: int32 [16, 2, 2, 1024], P('rows', 'rep'), may hold values from 0 to 127, as said below
- relation_ids: int32 [16, 2, 2], P('rows', 'rep'), may hold values from 0 to 7
Outputs:
- entity_grad: bfloat16 [98304, 256], P(('rows', 'rep'))
- relation_grad: float32 [8, 256, 256], replicated
Inputs may be any that keep to these rules, and one draw needn't show every extreme that they name: `send_offsets`: along the last dimension the offsets start at 0 and rise by 2 to 8 from owner to owner; there is one owner, the same for every device, from which every device requests exactly 8 rows (rise of 8), and there is one device that requests 8 rows from every owner. `source_ids`: each id is below the device's last entry of send_offsets; on every device some id is 0 and some id is that last entry minus 1. `target_ids`: each id is below the device's last entry of send_offsets; on every device some id is 0 and some id is that last entry minus 1. `negative_ids`: each id is below the device's last entry of send_offsets; on every device some id is 0 and some id is that last entry minus 1. `need_rows`: entries past an owner's count of requested rows are not referenced.
All inputs are finite; a program needn't handle non-finite values.
Results may differ from a plain program's by a relative error of at most 0.0065.
Values may be sent and summed in bfloat16 or wider, within the bound.
A program may use at most 64 MiB of HBM per device.

v0:
```python
import jax
import jax.numpy as jnp
from jax import lax
from jax.sharding import PartitionSpec as P


def locate(edge_ids, offsets, capacity):
    upper_bound = offsets[1:]
    lower_bound = offsets[:-1]
    owner_index = jnp.sum((edge_ids[..., None] >= upper_bound).astype(jnp.int32), axis=-1)
    start_slot = jnp.max(jnp.where(edge_ids[..., None] >= lower_bound, lower_bound, 0), axis=-1)
    return owner_index * capacity + edge_ids - start_slot


def block_terms(source, target, negative, operator, weight_neg):
    query = jnp.dot(source, operator, preferred_element_type=jnp.float32).astype(jnp.bfloat16)
    positive = jnp.einsum("bd,bd->b", query, target, preferred_element_type=jnp.float32)
    scores = jnp.einsum("bd,nd->bn", query, negative, preferred_element_type=jnp.float32)
    slope = -jax.nn.sigmoid(-positive)
    neg_weight = (jax.nn.sigmoid(scores) * weight_neg).astype(jnp.bfloat16)
    query_grad = slope[:, None] * target.astype(jnp.float32) + jnp.dot(
        neg_weight, negative, preferred_element_type=jnp.float32
    )
    query_grad = query_grad.astype(jnp.bfloat16)
    target_grad = slope[:, None] * query.astype(jnp.float32)
    negative_grad = jnp.einsum("bn,bd->nd", neg_weight, query, preferred_element_type=jnp.float32)
    source_grad = jnp.einsum("bd,ed->be", query_grad, operator, preferred_element_type=jnp.float32)
    operator_grad = jnp.einsum("be,bd->ed", source, query_grad, preferred_element_type=jnp.float32)
    return (source_grad, target_grad, negative_grad, operator_grad)


def shards(
    entity_table,
    relation_ops,
    need_rows,
    send_offsets,
    source_ids,
    target_ids,
    negative_ids,
    relation_ids,
):
    requests = need_rows[0, 0]
    owner_count, capacity = requests.shape
    row_width = entity_table.shape[1]
    received = lax.all_to_all(requests, "rows", split_axis=0, concat_axis=0, tiled=True)
    serve_picked = jnp.take(entity_table, received, axis=0)
    returned = lax.all_to_all(serve_picked, "rows", split_axis=0, concat_axis=0, tiled=True)
    fetched = returned
    slot_count = owner_count * capacity
    slots = fetched.reshape(slot_count, row_width)
    offsets = send_offsets[0, 0]
    source_slot = locate(source_ids[0, 0], offsets, capacity)
    target_slot = locate(target_ids[0, 0], offsets, capacity)
    negative_slot = locate(negative_ids[0, 0], offsets, capacity)
    relations = relation_ids[0, 0]
    edge_count = source_ids.shape[-1]
    weight_neg = negative_ids.shape[-1] ** (-0.5)
    slot_lane = jnp.arange(slot_count, dtype=jnp.int32)
    relation_lane = jnp.arange(relation_ops.shape[0], dtype=jnp.int32)
    slot_grad = jnp.zeros((slot_count, row_width), jnp.float32)
    operator_acc = jnp.zeros(relation_ops.shape, jnp.float32)
    for block_index in range(relations.shape[0]):
        joined_slot = jnp.concatenate(
            [source_slot[block_index], target_slot[block_index], negative_slot[block_index]], axis=0
        )
        picker = (joined_slot[:, None] == slot_lane[None, :]).astype(jnp.bfloat16)
        picked = jnp.dot(picker, slots, preferred_element_type=jnp.float32).astype(jnp.bfloat16)
        source = picked[:edge_count]
        target = picked[edge_count : 2 * edge_count]
        negative = picked[2 * edge_count :]
        operator = lax.dynamic_index_in_dim(relation_ops, relations[block_index], 0, keepdims=False)
        source_grad, target_grad, negative_grad, operator_grad = block_terms(
            source, target, negative, operator, weight_neg
        )
        joined_grad = jnp.concatenate([source_grad, target_grad, negative_grad], axis=0)
        upper_part = joined_grad.astype(jnp.bfloat16)
        lower_part = (joined_grad - upper_part.astype(jnp.float32)).astype(jnp.bfloat16)
        slot_grad = slot_grad + jnp.einsum(
            "rs,rd->sd", picker, upper_part, preferred_element_type=jnp.float32
        )
        slot_grad = slot_grad + jnp.einsum(
            "rs,rd->sd", picker, lower_part, preferred_element_type=jnp.float32
        )
        chosen = (relation_lane == relations[block_index]).astype(jnp.float32)
        operator_acc = operator_acc + chosen[:, None, None] * operator_grad[None, :, :]
    operator_total = lax.psum(operator_acc, ("rows", "rep"))
    devices = lax.axis_size("rows") * lax.axis_size("rep")
    relation_grad = (
        operator_total
        * (relation_ops.shape[0] / (edge_count * relations.shape[0] * devices)) ** 0.5
    )
    returned = lax.all_to_all(
        slot_grad.reshape(owner_count, capacity, row_width),
        "rows",
        split_axis=0,
        concat_axis=0,
        tiled=True,
    )
    flat_index = received.reshape(-1)
    flat_grad = returned.reshape(-1, row_width)
    owner_slab = (
        jnp.zeros((entity_table.shape[0], row_width), jnp.float32).at[flat_index].add(flat_grad)
    )
    entity_grad = lax.psum_scatter(owner_slab, "rep", scatter_dimension=0, tiled=True)
    return (entity_grad.astype(jnp.bfloat16), relation_grad)


def solution(mesh):
    return jax.shard_map(
        shards,
        mesh=mesh,
        in_specs=(
            P("rows", None),
            P(),
            P("rows", "rep", None, None),
            P("rows", "rep", None),
            P("rows", "rep", None, None),
            P("rows", "rep", None, None),
            P("rows", "rep", None, None),
            P("rows", "rep", None),
        ),
        out_specs=(P(("rows", "rep"), None), P()),
        check_vma=False,
    )
```

profile of v0, /device:TPU:0, one launch (start us, length us, event | category | flops | bytes accessed | tf_op | source)
XLA Modules:
  0.0 207.0 jit_solution(2638052348424822502)
XLA Ops:
  8.0 0.0 copy-start
  8.0 1.5 copy.21
  9.5 8.3 %all-to-all-start = ((s32[16,1,8]{2,1,0:T(1,128)}), s32[16,1,8]{2,1,0:T(1,128)S(1)}, u32[]{:S(2)}, u32[]{:S(2)}) async-start(s32[16,1,8]{2,1,0:T(1,128)} %copy.21), calls=%async_computation | async-start | bytes 16384 | tf_op jit(solution)/shard_map/all_to_all | solution.py:45
  17.8 0.8 slice_bitcast_fusion
  18.6 1.0 convert_reduce_fusion
  19.7 0.7 add_subtract_fusion
  20.4 0.7 add_subtract_fusion.2
  21.2 1.4 fusion.69
  22.6 2.5 %all-to-all-done = s32[16,1,8]{2,1,0:T(1,128)S(1)} async-done(((s32[16,1,8]{2,1,0:T(1,128)}), s32[16,1,8]{2,1,0:T(1,128)S(1)}, u32[]{:S(2)}, u32[]{:S(2)}) %all-to-all-start) | async-done | bytes 544 | tf_op jit(solution)/shard_map/all_to_all | solution.py:45
  25.0 0.1 copy.22
  25.1 0.1 copy.23
  25.2 0.1 copy.25
  25.3 0.1 reshape.115
  25.4 0.0 copy-done
  25.4 0.8 gather_fusion
  26.2 0.7 bitcast_select_fusion
  27.0 4.4 %all-to-all-start.1 = ((bf16[16,8,256]{2,1,0:T(8,128)(2,1)}), bf16[16,8,256]{2,1,0:T(8,128)(2,1)S(1)}, u32[]{:S(2)}, u32[]{:S(2)}) async-start(bf16[16,8,256]{2,1,0:T(8,128)(2,1)} %bitcast_select_fusion), calls=%async_computation.1 | async-start | bytes 131072 | tf_op jit(solution)/shard_map/all_to_all | solution.py:47
  31.4 0.0 all-reduce.2.cloned.1.call-start
  31.4 1.3 compare_convert_fusion
  36.8 2.1 %all-to-all-done.1 = bf16[16,8,256]{2,1,0:T(8,128)(2,1)S(1)} async-done(((bf16[16,8,256]{2,1,0:T(8,128)(2,1)}), bf16[16,8,256]{2,1,0:T(8,128)(2,1)S(1)}, u32[]{:S(2)}, u32[]{:S(2)}) %all-to-all-start.1) | async-done | bytes 65568 | tf_op jit(solution)/shard_map/all_to_all | solution.py:47
  38.9 1.6 convolution_convert_fusion.1
  40.6 1.3 fusion.26
  41.9 0.0 copy-start.3
  41.9 1.3 multiply_convert_fusion.1
  43.2 0.0 copy-done.3
  43.2 0.0 copy-start.4
  43.2 1.3 convert_multiply_fusion.2
  44.5 0.7 fusion.12
  45.3 0.0 copy-done.4
  45.3 0.3 fusion.41
  45.6 2.2 %fusion.48 = f32[1024,256]{1,0:T(8,128)} fusion(bf16[1024,256]{1,0:T(8,128)(2,1)S(1)} %fusion.12, bf16[8,256,256]{2,1,0:T(8,128)(2,1)} %param.9, s32[]{:T(128)S(6)} %select_n.54), kind=kOutput, calls=%fused_computation.60 | convolution fusion | flops 134217728 | bytes 1703940 | tf_op jit(solution)/shard_map/bd,ed->be/dot_general | solution.py:27
  47.9 1.8 convolution_convert_fusion
  49.7 1.3 fusion.27
  51.0 1.3 multiply_convert_fusion
  52.3 0.2 convert_multiply_fusion
  52.5 0.7 fusion.13
  53.2 0.7 fusion.71
  54.0 0.3 fusion.36
  54.3 1.2 fusion.45
  55.6 1.1 fusion.4
  56.6 1.1 fusion.5
  57.7 1.7 multiply_add_fusion
  59.4 0.0 all-reduce.2.cloned.1.call-update
  59.5 0.0 copy-start.1
  59.5 0.0 copy-start.2
  59.5 2.6 %fusion.70 = f32[1024,256]{1,0:T(8,128)S(1)} fusion(bf16[1024,1024]{1,0:T(8,128)(2,1)} %copy-done.4, bf16[1024,256]{1,0:T(8,128)(2,1)} %copy-done.3), kind=kOutput, calls=%fused_computation.105 | convolution fusion | flops 536870912 | bytes 3670016 | tf_op jit(solution)/shard_map/bn,bd->nd/dot_general | solution.py:26
  62.1 0.0 copy-done.1
  62.1 0.0 copy-done.2
  62.1 1.1 fusion.6
  63.1 1.7 fusion.23
  64.9 4.8 %all-to-all-start.2 = ((f32[16,8,256]{2,1,0:T(8,128)}), f32[16,8,256]{2,1,0:T(8,128)S(1)}, u32[]{:S(2)}, u32[]{:S(2)}) async-start(f32[16,8,256]{2,1,0:T(8,128)} %fusion.23), calls=%async_computation.2 | async-start | bytes 262144 | tf_op jit(solution)/shard_map/all_to_all | solution.py:92
  69.7 0.0 reduce-scatter.2.cloned.1.call-start
  69.8 0.5 broadcast.84
  70.3 0.7 reduce.7
  71.0 0.1 reshape.109
  71.0 6.8 %all-to-all-done.2 = f32[16,8,256]{2,1,0:T(8,128)S(1)} async-done(((f32[16,8,256]{2,1,0:T(8,128)}), f32[16,8,256]{2,1,0:T(8,128)S(1)}, u32[]{:S(2)}, u32[]{:S(2)}) %all-to-all-start.2) | async-done | bytes 131104 | tf_op jit(solution)/shard_map/all_to_all | solution.py:92
  77.9 4.3 %scatter_custom_fusion = f32[6144,256]{1,0:T(8,128)} fusion(s32[128]{0:T(128)S(1)} %fusion.57, f32[]{:T(128)} %constant.10.clone.1, f32[16,8,256]{2,1,0:T(8,128)S(1)} %all-to-all-done.2), kind=kCustom, calls=%fused_computation.10 | custom fusion | flops 32768 | bytes 6422532 | tf_op jit(solution)/shard_map/scatter-add | solution.py:102
  82.2 0.0 reduce-scatter.2.cloned.1.call-update
  82.2 111.1 %all-reduce.2.cloned.1.call-done = f32[8,256,256]{2,1,0:T(8,128)} async-done(((f32[8,256,256]{2,1,0:T(8,128)}), f32[8,256,256]{2,1,0:T(8,128)}) %all-reduce.2.cloned.1.call-update) | async-done | bytes 2097168 | tf_op jit(solution)/shard_map/psum | solution.py:86
  193.3 3.1 %broadcast_multiply_fusion = f32[8,256,256]{2,1,0:T(8,128)} fusion(f32[8,256,256]{2,1,0:T(8,128)} %all-reduce.2.cloned.1.call-done), kind=kLoop, calls=%fused_computation.39 | loop fusion | flops 524288 | bytes 4194304 | tf_op jit(solution)/shard_map/mul | solution.py:89
  196.4 0.0 reduce-scatter.2.cloned.1.call-done
  196.4 3.2 %convert_element_type.103 = bf16[3072,256]{1,0:T(8,128)(2,1)} convert(f32[3072,256]{1,0:T(8,128)} %reduce-scatter.2.cloned.1.call-done) | non-fusion elementwise | flops 786432 | bytes 4718592 | tf_op jit(solution)/shard_map/convert_element_type | solution.py:105
  (11 shorter events, 0.1 us)
Async XLA Ops:
  8.0 17.4 %copy-start = (bf16[6144,256]{1,0:T(8,128)(2,1)S(1)}, bf16[6144,256]{1,0:T(8,128)(2,1)}, u32[]{:S(2)}) copy-start(bf16[6144,256]{1,0:T(8,128)(2,1)} %param.8) | copy-start | bytes 9437188
  9.5 15.5 %all-to-all-start = ((s32[16,1,8]{2,1,0:T(1,128)}), s32[16,1,8]{2,1,0:T(1,128)S(1)}, u32[]{:S(2)}, u32[]{:S(2)}) async-start(s32[16,1,8]{2,1,0:T(1,128)} %copy.21), calls=%async_computation | async-start | bytes 16384 | tf_op jit(solution)/shard_map/all_to_all | solution.py:45
  27.0 12.0 %all-to-all-start.1 = ((bf16[16,8,256]{2,1,0:T(8,128)(2,1)}), bf16[16,8,256]{2,1,0:T(8,128)(2,1)S(1)}, u32[]{:S(2)}, u32[]{:S(2)}) async-start(bf16[16,8,256]{2,1,0:T(8,128)(2,1)} %bitcast_select_fusion), calls=%async_computation.1 | async-start | bytes 131072 | tf_op jit(solution)/shard_map/all_to_all | solution.py:47
  31.4 161.9 %all-reduce.2.cloned.1.call-start = ((), (), s32[]{:S(2)}) async-start(), calls=%async_computation.5 | async-start | bytes 4194304 | tf_op jit(solution)/shard_map/psum | solution.py:86
  41.9 1.3 copy-start.3
  43.2 2.0 copy-start.4
  59.5 2.6 %copy-start.1 = (f32[1024,256]{1,0:T(8,128)S(1)}, f32[1024,256]{1,0:T(8,128)}, u32[]{:S(2)}) copy-start(f32[1024,256]{1,0:T(8,128)} %fusion.48) | copy-start | bytes 3145732
  59.5 2.6 %copy-start.2 = (f32[1024,256]{1,0:T(8,128)S(1)}, f32[1024,256]{1,0:T(8,128)}, u32[]{:S(2)}) copy-start(f32[1024,256]{1,0:T(8,128)} %convert_multiply_fusion.2) | copy-start | bytes 3145732
  64.9 13.0 %all-to-all-start.2 = ((f32[16,8,256]{2,1,0:T(8,128)}), f32[16,8,256]{2,1,0:T(8,128)S(1)}, u32[]{:S(2)}, u32[]{:S(2)}) async-start(f32[16,8,256]{2,1,0:T(8,128)} %fusion.23), calls=%async_computation.2 | async-start | bytes 262144 | tf_op jit(solution)/shard_map/all_to_all | solution.py:92
  69.7 126.7 %reduce-scatter.2.cloned.1.call-start = ((), (), s32[]{:S(2)}) async-start(), calls=%async_computation.4 | async-start | bytes 9437184 | tf_op jit(solution)/shard_map/reduce_scatter | solution.py:104
Sparse Core Ops, SparseCore 0:
  59.6 133.6 all-reduce.1
Sparse Core Ops, SparseCore 1:
  82.3 12.0 reduce-scatter.1
where the time goes:
time: 208 us; the launch traced here: 207 us
  waiting for transfers between devices  123 us (59%)
  matrix products  22.5 us (11%)
  between operations  19.8 us (10%)
  other arithmetic  19 us (9%)
  starting transfers between devices  17.6 us (8%)
  local copies, waits for them, and re-layouts  5.52 us (3%)
    psum x1, waiting for transfers between devices, shards(): operator_total = lax.psum(operator_acc, ('rows', 'rep'))  111 us
    all_to_all x1, starting transfers between devices, shards(): lax.all_to_all(requests, 'rows', split_axis=0, concat_axis=0, tiled=True)  8.31 us
    all_to_all x1, waiting for transfers between devices, shards(): lax.all_to_all(slot_grad.reshape(owner_count, capacity, row_width), 'rows...  6.83 us
    all_to_all x1, starting transfers between devices, shards(): lax.all_to_all(slot_grad.reshape(owner_count, capacity, row_width), 'rows...  4.82 us
    all_to_all x1, starting transfers between devices, shards(): lax.all_to_all(serve_picked, 'rows', split_axis=0, concat_axis=0, tiled=T...  4.43 us
    scatter-add x1, other arithmetic, shards(): jnp.zeros((entity_table.shape[0], row_width), jnp.float32).at[flat_index]  4.29 us
  transfers between devices with their start and end apart: 5, of which 4 were waited for; matrix products, arithmetic and copies ran while one was open for 10% of the time, Pallas kernels for 0%

commit v1 on v0

--- a/solution.py
+++ b/solution.py
@@ -83,7 +83,9 @@
         )
         chosen = (relation_lane == relations[block_index]).astype(jnp.float32)
         operator_acc = operator_acc + chosen[:, None, None] * operator_grad[None, :, :]
-    operator_total = lax.psum(operator_acc, ("rows", "rep"))
+    operator_total = operator_acc
+    for axis in ("rep", "rows"):
+        operator_total = lax.psum(operator_total, axis)
     devices = lax.axis_size("rows") * lax.axis_size("rep")
     relation_grad = (
         operator_total

time: 208 us -> 236 us (1.13)
  waiting for transfers between devices: 123 us -> 145 us
  matrix products: 22.5 us -> 25 us
    reduce_scatter x1, waiting for transfers between devices: 0.01 us -> 13.1 us  [shards(): lax.psum_scatter(owner_slab, 'rep', scatter_dimension=0, tiled=True)]
    psum x1 -> x2, waiting for transfers between devices: 111 us -> 118 us  [shards(): operator_total = lax.psum(operator_total, axis)]
    dot_general x2, matrix products: 2.8 us -> 5.4 us  [shards(): jnp.einsum('rs,rd->sd', picker, upper_part, preferred_element_type=jnp.fl...]
  transfers between devices with their start and end apart: 5 -> 6, of which waited for: 4 -> 6; matrix products, arithmetic and copies ran while one was open for 10% -> 13% of each run, Pallas kernels for 0% -> 0%
where the time goes in v1:
time: 236 us; the launch traced here: 235 us
  waiting for transfers between devices  145 us (61%)
  matrix products  25 us (11%)
  starting transfers between devices  19.8 us (8%)
  other arithmetic  19.8 us (8%)
  between operations  18.1 us (8%)
  local copies, waits for them, and re-layouts  7.76 us (3%)
    psum x2, waiting for transfers between devices, shards(): operator_total = lax.psum(operator_total, axis)  118 us
    reduce_scatter x1, waiting for transfers between devices, shards(): lax.psum_scatter(owner_slab, 'rep', scatter_dimension=0, tiled=True)  13.1 us
    all_to_all x1, waiting for transfers between devices, shards(): lax.all_to_all(slot_grad.reshape(owner_count, capacity, row_width), 'rows...  9.17 us
    all_to_all x1, starting transfers between devices, shards(): lax.all_to_all(requests, 'rows', split_axis=0, concat_axis=0, tiled=True)  8.31 us
    all_to_all x1, starting transfers between devices, shards(): lax.all_to_all(slot_grad.reshape(owner_count, capacity, row_width), 'rows...  6.79 us
    dot_general x2, matrix products, shards(): jnp.einsum('rs,rd->sd', picker, upper_part, preferred_element_type=jnp.fl...  5.4 us
  transfers between devices with their start and end apart: 6, of which 6 were waited for; matrix products, arithmetic and copies ran while one was open for 13% of the time, Pallas kernels for 0%

profile of v1, /device:TPU:0, one launch (start us, length us, event | category | flops | bytes accessed | tf_op | source)
XLA Modules:
  0.0 235.4 jit_solution(14973035856496258693)
XLA Ops:
  7.2 0.0 copy-start
  7.2 1.5 copy.21
  8.7 8.3 %all-to-all-start = ((s32[16,1,8]{2,1,0:T(1,128)}), s32[16,1,8]{2,1,0:T(1,128)S(1)}, u32[]{:S(2)}, u32[]{:S(2)}) async-start(s32[16,1,8]{2,1,0:T(1,128)} %copy.21), calls=%async_computation | async-start | bytes 16384 | tf_op jit(solution)/shard_map/all_to_all | solution.py:45
  17.0 0.8 slice_bitcast_fusion
  17.8 1.0 convert_reduce_fusion
  18.8 0.7 add_subtract_fusion
  19.6 0.7 add_subtract_fusion.2
  20.3 1.4 fusion.69
  21.7 2.5 %all-to-all-done = s32[16,1,8]{2,1,0:T(1,128)S(1)} async-done(((s32[16,1,8]{2,1,0:T(1,128)}), s32[16,1,8]{2,1,0:T(1,128)S(1)}, u32[]{:S(2)}, u32[]{:S(2)}) %all-to-all-start) | async-done | bytes 544 | tf_op jit(solution)/shard_map/all_to_all | solution.py:45
  24.2 0.1 copy.22
  24.3 0.1 copy.23
  24.4 0.1 copy.25
  24.4 0.1 reshape.115
  24.5 0.0 copy-done
  24.6 0.8 gather_fusion
  25.4 0.7 bitcast_select_fusion
  26.1 4.4 %all-to-all-start.1 = ((bf16[16,8,256]{2,1,0:T(8,128)(2,1)}), bf16[16,8,256]{2,1,0:T(8,128)(2,1)S(1)}, u32[]{:S(2)}, u32[]{:S(2)}) async-start(bf16[16,8,256]{2,1,0:T(8,128)(2,1)} %bitcast_select_fusion), calls=%async_computation.1 | async-start | bytes 131072 | tf_op jit(solution)/shard_map/all_to_all | solution.py:47
  30.6 0.0 all-reduce.3.cloned.1.call-start
  30.6 1.3 compare_convert_fusion
  36.0 2.1 all-to-all-done.1
  38.1 1.6 convolution_convert_fusion
  39.7 1.3 fusion.27
  41.1 1.6 convolution_convert_fusion.1
  42.7 1.3 fusion.26
  44.0 1.3 multiply_convert_fusion.1
  45.4 0.7 fusion.12
  46.1 0.6 copy-done.8
  46.7 0.3 fusion.41
  47.1 0.5 copy-done.5
  47.5 1.3 multiply_convert_fusion
  48.8 0.0 copy-start.10
  48.9 0.7 fusion.13
  49.6 0.6 copy-done.10
  50.2 0.3 fusion.36
  50.5 0.5 copy-done.7
  51.0 1.6 multiply_add_fusion
  52.6 0.0 all-reduce.3.cloned.1.call-update
  52.6 0.2 all-reduce.5.cloned.1.call-start
  52.8 2.2 convert_multiply_fusion
  55.1 3.4 %fusion.71 = f32[1024,256]{1,0:T(8,128)} fusion(bf16[1024,1024]{1,0:T(8,128)(2,1)} %copy-done.10, bf16[1024,256]{1,0:T(8,128)(2,1)} %copy-done.4), kind=kOutput, calls=%fused_computation.106 | convolution fusion | flops 536870912 | bytes 3670016 | tf_op jit(solution)/shard_map/bn,bd->nd/dot_general | solution.py:26
  58.4 14.8 %all-reduce.3.cloned.1.call-done = f32[8,256,256]{2,1,0:T(8,128)} async-done(((f32[8,256,256]{2,1,0:T(8,128)}), f32[8,256,256]{2,1,0:T(8,128)}) %all-reduce.3.cloned.1.call-update) | async-done | bytes 2097168 | tf_op jit(solution)/shard_map/psum | solution.py:88
  73.2 0.0 all-reduce.5.cloned.1.call-update
  73.2 1.4 fusion.45
  74.6 0.0 copy-start.11
  74.6 3.6 %fusion.5 = f32[128,256]{1,0:T(8,128)S(1)} fusion(f32[1024,256]{1,0:T(8,128)} %fusion.71, f32[1024,256]{1,0:T(8,128)} %convert_multiply_fusion, f32[1024,256]{1,0:T(8,128)S(1)} %fusion.45, s32[3072]{0:T(1024)S(1)} %pad_add_fusion.1), kind=kOutput, calls=%fused_computation.17 | convolution fusion | flops 206438400 | bytes 3289088 | tf_op jit(solution)/shard_map/rs,rd->sd/dot_general | solution.py:78
  78.3 1.1 fusion.4
  79.4 1.4 fusion.48
  80.8 0.2 convert_multiply_fusion.2
  81.0 0.1 copy-done.9
  81.1 0.8 fusion.70
  81.9 1.1 fusion.6
  82.9 1.8 fusion.23
  84.7 6.8 %all-to-all-start.2 = ((f32[16,8,256]{2,1,0:T(8,128)}), f32[16,8,256]{2,1,0:T(8,128)S(1)}, u32[]{:S(2)}, u32[]{:S(2)}) async-start(f32[16,8,256]{2,1,0:T(8,128)} %fusion.23), calls=%async_computation.2 | async-start | bytes 262144 | tf_op jit(solution)/shard_map/all_to_all | solution.py:94
  91.5 0.0 reduce-scatter.2.cloned.1.call-start
  91.6 0.5 broadcast.84
  92.1 0.7 reduce.7
  92.7 0.1 reshape.109
  92.8 9.2 %all-to-all-done.2 = f32[16,8,256]{2,1,0:T(8,128)S(1)} async-done(((f32[16,8,256]{2,1,0:T(8,128)}), f32[16,8,256]{2,1,0:T(8,128)S(1)}, u32[]{:S(2)}, u32[]{:S(2)}) %all-to-all-start.2) | async-done | bytes 131104 | tf_op jit(solution)/shard_map/all_to_all | solution.py:94
  102.0 4.3 %scatter_custom_fusion = f32[6144,256]{1,0:T(8,128)} fusion(s32[128]{0:T(128)S(1)} %fusion.57, f32[]{:T(128)} %constant.10.clone.1, f32[16,8,256]{2,1,0:T(8,128)S(1)} %all-to-all-done.2), kind=kCustom, calls=%fused_computation.10 | custom fusion | flops 32768 | bytes 6422532 | tf_op jit(solution)/shard_map/scatter-add | solution.py:104
  106.3 0.0 reduce-scatter.2.cloned.1.call-update
  106.3 103.1 %all-reduce.5.cloned.1.call-done = f32[8,256,256]{2,1,0:T(8,128)} async-done(((f32[8,256,256]{2,1,0:T(8,128)}), f32[8,256,256]{2,1,0:T(8,128)}) %all-reduce.5.cloned.1.call-update) | async-done | bytes 2097168 | tf_op jit(solution)/shard_map/psum | solution.py:88
  209.5 3.1 %broadcast_multiply_fusion = f32[8,256,256]{2,1,0:T(8,128)} fusion(f32[8,256,256]{2,1,0:T(8,128)} %all-reduce.5.cloned.1.call-done), kind=kLoop, calls=%fused_computation.39 | loop fusion | flops 524288 | bytes 4194304 | tf_op jit(solution)/shard_map/mul | solution.py:91
  212.6 13.1 %reduce-scatter.2.cloned.1.call-done = f32[3072,256]{1,0:T(8,128)} async-done(((f32[6144,256]{1,0:T(8,128)}), f32[3072,256]{1,0:T(8,128)}) %reduce-scatter.2.cloned.1.call-update) | async-done | bytes 3145744 | tf_op jit(solution)/shard_map/reduce_scatter | solution.py:106
  225.7 3.2 %convert_element_type.103 = bf16[3072,256]{1,0:T(8,128)(2,1)} convert(f32[3072,256]{1,0:T(8,128)} %reduce-scatter.2.cloned.1.call-done) | non-fusion elementwise | flops 786432 | bytes 4718592 | tf_op jit(solution)/shard_map/convert_element_type | solution.py:107
  (26 shorter events, 0.1 us)
Async XLA Ops:
  7.2 17.4 %copy-start = (bf16[6144,256]{1,0:T(8,128)(2,1)S(1)}, bf16[6144,256]{1,0:T(8,128)(2,1)}, u32[]{:S(2)}) copy-start(bf16[6144,256]{1,0:T(8,128)(2,1)} %param.8) | copy-start | bytes 9437188
  8.7 15.5 %all-to-all-start = ((s32[16,1,8]{2,1,0:T(1,128)}), s32[16,1,8]{2,1,0:T(1,128)S(1)}, u32[]{:S(2)}, u32[]{:S(2)}) async-start(s32[16,1,8]{2,1,0:T(1,128)} %copy.21), calls=%async_computation | async-start | bytes 16384 | tf_op jit(solution)/shard_map/all_to_all | solution.py:45
  26.1 12.0 %all-to-all-start.1 = ((bf16[16,8,256]{2,1,0:T(8,128)(2,1)}), bf16[16,8,256]{2,1,0:T(8,128)(2,1)S(1)}, u32[]{:S(2)}, u32[]{:S(2)}) async-start(bf16[16,8,256]{2,1,0:T(8,128)(2,1)} %bitcast_select_fusion), calls=%async_computation.1 | async-start | bytes 131072 | tf_op jit(solution)/shard_map/all_to_all | solution.py:47
  30.6 42.6 %all-reduce.3.cloned.1.call-start = ((), (), s32[]{:S(2)}) async-start(), calls=%async_computation.5 | async-start | bytes 4194304 | tf_op jit(solution)/shard_map/psum | solution.py:88
  41.0 6.5 %copy-start.4 = (bf16[1024,256]{1,0:T(8,128)(2,1)}, bf16[1024,256]{1,0:T(8,128)(2,1)S(1)}, u32[]{:S(2)}) copy-start(bf16[1024,256]{1,0:T(8,128)(2,1)S(1)} %get-tuple-element.23) | copy-start | bytes 1572868
  44.0 1.3 copy-start.2
  45.4 1.4 copy-start.8
  46.7 0.8 copy-start.5
  48.8 1.3 copy-start.10
  50.2 0.8 copy-start.7
  52.6 156.9 %all-reduce.5.cloned.1.call-start = ((), (), s32[]{:S(2)}) async-start(), calls=%async_computation.6 | async-start | bytes 4194304 | tf_op jit(solution)/shard_map/psum | solution.py:88
  74.6 3.7 %copy-start.1 = (f32[1024,256]{1,0:T(8,128)S(1)}, f32[1024,256]{1,0:T(8,128)}, u32[]{:S(2)}) copy-start(f32[1024,256]{1,0:T(8,128)} %convert_multiply_fusion) | copy-start | bytes 3145732
  74.6 3.7 %copy-start.11 = (f32[1024,256]{1,0:T(8,128)S(1)}, f32[1024,256]{1,0:T(8,128)}, u32[]{:S(2)}) copy-start(f32[1024,256]{1,0:T(8,128)} %fusion.71) | copy-start | bytes 3145732
  78.3 1.1 copy-start.6
  78.3 2.5 %copy-start.3 = (bf16[1024,256]{1,0:T(8,128)(2,1)S(1)}, bf16[1024,256]{1,0:T(8,128)(2,1)}, u32[]{:S(2)}) copy-start(bf16[1024,256]{1,0:T(8,128)(2,1)} %copy-done.2) | copy-start | bytes 1572868
  79.4 1.7 copy-start.9
  84.7 17.3 %all-to-all-start.2 = ((f32[16,8,256]{2,1,0:T(8,128)}), f32[16,8,256]{2,1,0:T(8,128)S(1)}, u32[]{:S(2)}, u32[]{:S(2)}) async-start(f32[16,8,256]{2,1,0:T(8,128)} %fusion.23), calls=%async_computation.2 | async-start | bytes 262144 | tf_op jit(solution)/shard_map/all_to_all | solution.py:94
  91.5 134.1 %reduce-scatter.2.cloned.1.call-start = ((), (), s32[]{:S(2)}) async-start(), calls=%async_computation.4 | async-start | bytes 9437184 | tf_op jit(solution)/shard_map/reduce_scatter | solution.py:106
Sparse Core Ops, SparseCore 0:
  52.7 20.4 all-reduce.2
  79.6 129.8 all-reduce.4
  211.8 13.8 reduce-scatter.1
